TPU v7x, 128 devices: a whole 4x4x4 slice. The times are simulated.
128 devices in a mesh: ctx: 32 (over x, y, core), head: 4 (over z).
Axes of the slice: x: 4, y: 4, z: 4, core: 2. Of those that a mesh axis runs over, the one named last changes fastest.
Arguments:
- query: bfloat16 [4, 8192], P(None, 'head'), may hold values from -8 to 8
- key_cache: bfloat16 [4, 131072, 1024], P(None, 'ctx', 'head'), may hold values from -80 to 80
- cached_value_matrix: bfloat16 [4, 131072, 1024], P(None, 'ctx', 'head'), may hold values from -24 to 24
- lengths: int32 [4], replicated, may hold values from 2 to 131072, as said below
- out_weight: bfloat16 [8192, 8192], P('head', 'ctx'), may hold values from -0.0625 to 0.0625
Outputs:
- projected: float32 [4, 8192], P(None, 'ctx')
Inputs may be any that keep to these rules, and one draw needn't show every extreme that they name: `lengths`: some sequence has exactly 131072 valid positions in every draw.
All inputs are finite; a program needn't handle non-finite values.
Results may differ from a plain program's by a relative error of at most 0.0095.
Values sent between devices are 32-bit elements; how exact they have to be, the bound alone decides.
No kernel may reach another device: no remote copies, remote signals or barrier semaphores. Data moves between devices by JAX's collectives and lax.ppermute only.
A program may use at most 64 MiB of HBM per device.

v0:
```python
import jax
import jax.numpy as jnp
from jax import lax
from jax.sharding import PartitionSpec as P

HEAD_WIDTH = 128


def combine_pair(first, second):
    mixed_a, top_a, total_a = first
    mixed_b, top_b, total_b = second
    top = jnp.maximum(top_a, top_b)
    scale_b = jnp.exp(top_b - top)
    return (mixed_b * scale_b[..., None], top, total_b * scale_b)


def fold_pieces(carry, pieces):
    mixed_p, top_p, total_p = pieces
    piece_top = jnp.max(top_p, axis=0)
    scales = jnp.exp(top_p - piece_top[None])
    folded = (
        jnp.sum(mixed_p * scales[..., None], axis=0),
        piece_top,
        jnp.sum(total_p * scales, axis=0),
    )
    return combine_pair(carry, folded)


def on_device(query, key_cache, cached_value_matrix, lengths, out_weight):
    rows, ctx_dev, kv_cols = key_cache.shape
    kv_heads = kv_cols // HEAD_WIDTH
    q_heads = query.shape[1] // HEAD_WIDTH
    query_group = q_heads // kv_heads
    span = 512
    blocks = ctx_dev // span
    offset = lax.axis_index("ctx") * ctx_dev
    query_rows = query.reshape(rows, kv_heads, query_group, HEAD_WIDTH)
    scale = 1.0 / jnp.sqrt(jnp.float32(HEAD_WIDTH))

    def step(index, carry):
        mixed, top, total = carry
        key_block = lax.dynamic_slice_in_dim(key_cache, index * span, span, 1).reshape(
            rows, span, kv_heads, HEAD_WIDTH
        )
        value_block = lax.dynamic_slice_in_dim(cached_value_matrix, index * span, span, 1).reshape(
            rows, span, kv_heads, HEAD_WIDTH
        )
        scores = (
            jnp.einsum("rgjd,rcgd->rgjc", query_rows, key_block, preferred_element_type=jnp.float32)
            * scale
        )
        places = offset + index * span + jnp.arange(span, dtype=jnp.int32)
        valid = (places[None, :] < lengths[:, None])[:, None, None, :]
        new_top = jnp.maximum(top, jnp.max(jnp.where(valid, scores, jnp.float32(-1e30)), axis=-1))
        weights = jnp.where(valid, jnp.exp(scores - new_top[..., None]), jnp.float32(0.0))
        factor = jnp.exp(top - new_top)
        total = total * factor + jnp.sum(weights, axis=-1)
        update = jnp.einsum(
            "rgjc,rcgd->rgjd",
            weights.astype(jnp.bfloat16),
            value_block,
            preferred_element_type=jnp.float32,
        )
        return (mixed * factor[..., None] + update, new_top, total)

    start_state = (
        jnp.zeros((rows, kv_heads, query_group, HEAD_WIDTH), jnp.float32),
        jnp.full((rows, kv_heads, query_group), -1e30, jnp.float32),
        jnp.zeros((rows, kv_heads, query_group), jnp.float32),
    )
    mixed, top, total = lax.fori_loop(0, blocks, step, start_state)
    mixed, top, total = fold_pieces(
        start_state,
        (
            lax.all_gather(mixed[None], "ctx", axis=0, tiled=True),
            lax.all_gather(top[None], "ctx", axis=0, tiled=True),
            lax.all_gather(total[None], "ctx", axis=0, tiled=True),
        ),
    )
    attended = (mixed / total[..., None]).astype(jnp.bfloat16).reshape(rows, q_heads * HEAD_WIDTH)
    partial_value = jnp.dot(attended, out_weight, preferred_element_type=jnp.float32)
    return lax.psum(partial_value, "head")


def solution(mesh):
    in_specs = (
        P(None, "head"),
        P(None, "ctx", "head"),
        P(None, "ctx", "head"),
        P(),
        P("head", "ctx"),
    )
    out_specs = P(None, "ctx")
    return jax.shard_map(
        on_device, mesh=mesh, in_specs=in_specs, out_specs=out_specs, check_vma=False
    )
```

profile of v0, /device:TPU:0, one launch (start us, length us, event | category | flops | bytes accessed | tf_op | source)
XLA Modules:
  0.0 130.4 jit_solution(4136145605746691784)
XLA Ops:
  6.5 0.8 copy.25
  7.4 52.1 %while.18 = (s32[]{:T(128)}, f32[4,2,8,128]{3,2,1,0:T(8,128)S(1)}, f32[4,2,8]{2,1,0:T(2,128)S(1)}, f32[4,2,8]{2,1,0:T(2,128)S(1)}, s32[]{:T(128)}, /*index=5*/s3...) while((s32[]{:T(128)}, f32[4,2,8,128]{3,2,1,0:T(8,128)S(1)}, ...), condition=%wide.region_3.4_spmd.clone, body=%wide.region_0.3_spmd.clone.sunk | while | flops 17099592 | bytes 10977499 | solution.py:71
  7.4 1.7 %constant_dynamic-slice_fusion.3 = (bf16[4,512,256]{2,1,0:T(8,128)(2,1)S(1)}, bf16[4,512,256]{2,1,0:T(8,128)(2,1)S(1)}) fusion(bf16[4,4096,256]{2,1,0:T(8,128)(2,1)} %get-tuple-element.339, s32[]{:T(128)S(6)} %select_n.45, bf16[4,4096,256]{2,1,0:T(8,128)(2,1)} %get-tuple-element.337), kind=kLoop, calls=%fused_computation.17.clone.1 | loop fusion | bytes 4194308 | tf_op jit(solution)/shard_map/while/body/eval_jaxpr/dynamic_slice | solution.py:45
  9.0 1.3 %copy.29 = bf16[4,512,256]{1,2,0:T(8,128)(2,1)} copy(bf16[4,512,256]{2,1,0:T(8,128)(2,1)S(1)} %get-tuple-element.300) | data formatting | bytes 2097152 | tf_op jit(solution)/shard_map/while/body/eval_jaxpr/dynamic_slice | solution.py:42
  10.4 0.7 broadcast_compare_fusion.2
  11.1 1.6 %select_reduce_fusion.2 = (f32[4,2,8]{2,1,0:T(2,128)S(1)}, f32[4,2,512,8]{2,3,1,0:T(8,128)S(1)}) fusion(pred[4,512]{1,0:T(4,128)(4,1)S(1)} %broadcast_compare_fusion.2, bf16[4,512,2,128]{1,3,2,0:T(8,128)(2,1)} %bitcast.39, bf16[4,2,8,128]{3,2,1,0:T(8,128)(2,1)S(1)} %get-tuple-element.338), kind=kOutput, calls=%fused_computation.5.clone.1 | convolution fusion | flops 8486848 | bytes 1198336 | tf_op jit(solution)/shard_map/while/body/eval_jaxpr/rgjd,rcgd->rgjc/dot_general | solution.py:49
  13.9 1.7 %constant_dynamic-slice_fusion.3 = (bf16[4,512,256]{2,1,0:T(8,128)(2,1)S(1)}, bf16[4,512,256]{2,1,0:T(8,128)(2,1)S(1)}) fusion(bf16[4,4096,256]{2,1,0:T(8,128)(2,1)} %get-tuple-element.339, s32[]{:T(128)S(6)} %select_n.45, bf16[4,4096,256]{2,1,0:T(8,128)(2,1)} %get-tuple-element.337), kind=kLoop, calls=%fused_computation.17.clone.1 | loop fusion | bytes 4194308 | tf_op jit(solution)/shard_map/while/body/eval_jaxpr/dynamic_slice | solution.py:45
  15.6 1.3 %copy.29 = bf16[4,512,256]{1,2,0:T(8,128)(2,1)} copy(bf16[4,512,256]{2,1,0:T(8,128)(2,1)S(1)} %get-tuple-element.300) | data formatting | bytes 2097152 | tf_op jit(solution)/shard_map/while/body/eval_jaxpr/dynamic_slice | solution.py:42
  17.6 1.6 %select_reduce_fusion.2 = (f32[4,2,8]{2,1,0:T(2,128)S(1)}, f32[4,2,512,8]{2,3,1,0:T(8,128)S(1)}) fusion(pred[4,512]{1,0:T(4,128)(4,1)S(1)} %broadcast_compare_fusion.2, bf16[4,512,2,128]{1,3,2,0:T(8,128)(2,1)} %bitcast.39, bf16[4,2,8,128]{3,2,1,0:T(8,128)(2,1)S(1)} %get-tuple-element.338), kind=kOutput, calls=%fused_computation.5.clone.1 | convolution fusion | flops 8486848 | bytes 1198336 | tf_op jit(solution)/shard_map/while/body/eval_jaxpr/rgjd,rcgd->rgjc/dot_general | solution.py:49
  20.4 1.7 %constant_dynamic-slice_fusion.3 = (bf16[4,512,256]{2,1,0:T(8,128)(2,1)S(1)}, bf16[4,512,256]{2,1,0:T(8,128)(2,1)S(1)}) fusion(bf16[4,4096,256]{2,1,0:T(8,128)(2,1)} %get-tuple-element.339, s32[]{:T(128)S(6)} %select_n.45, bf16[4,4096,256]{2,1,0:T(8,128)(2,1)} %get-tuple-element.337), kind=kLoop, calls=%fused_computation.17.clone.1 | loop fusion | bytes 4194308 | tf_op jit(solution)/shard_map/while/body/eval_jaxpr/dynamic_slice | solution.py:45
  22.1 1.3 %copy.29 = bf16[4,512,256]{1,2,0:T(8,128)(2,1)} copy(bf16[4,512,256]{2,1,0:T(8,128)(2,1)S(1)} %get-tuple-element.300) | data formatting | bytes 2097152 | tf_op jit(solution)/shard_map/while/body/eval_jaxpr/dynamic_slice | solution.py:42
  23.4 0.7 broadcast_compare_fusion.2
  24.1 1.6 %select_reduce_fusion.2 = (f32[4,2,8]{2,1,0:T(2,128)S(1)}, f32[4,2,512,8]{2,3,1,0:T(8,128)S(1)}) fusion(pred[4,512]{1,0:T(4,128)(4,1)S(1)} %broadcast_compare_fusion.2, bf16[4,512,2,128]{1,3,2,0:T(8,128)(2,1)} %bitcast.39, bf16[4,2,8,128]{3,2,1,0:T(8,128)(2,1)S(1)} %get-tuple-element.338), kind=kOutput, calls=%fused_computation.5.clone.1 | convolution fusion | flops 8486848 | bytes 1198336 | tf_op jit(solution)/shard_map/while/body/eval_jaxpr/rgjd,rcgd->rgjc/dot_general | solution.py:49
  26.9 1.7 %constant_dynamic-slice_fusion.3 = (bf16[4,512,256]{2,1,0:T(8,128)(2,1)S(1)}, bf16[4,512,256]{2,1,0:T(8,128)(2,1)S(1)}) fusion(bf16[4,4096,256]{2,1,0:T(8,128)(2,1)} %get-tuple-element.339, s32[]{:T(128)S(6)} %select_n.45, bf16[4,4096,256]{2,1,0:T(8,128)(2,1)} %get-tuple-element.337), kind=kLoop, calls=%fused_computation.17.clone.1 | loop fusion | bytes 4194308 | tf_op jit(solution)/shard_map/while/body/eval_jaxpr/dynamic_slice | solution.py:45
  28.6 1.3 %copy.29 = bf16[4,512,256]{1,2,0:T(8,128)(2,1)} copy(bf16[4,512,256]{2,1,0:T(8,128)(2,1)S(1)} %get-tuple-element.300) | data formatting | bytes 2097152 | tf_op jit(solution)/shard_map/while/body/eval_jaxpr/dynamic_slice | solution.py:42
  30.7 1.6 %select_reduce_fusion.2 = (f32[4,2,8]{2,1,0:T(2,128)S(1)}, f32[4,2,512,8]{2,3,1,0:T(8,128)S(1)}) fusion(pred[4,512]{1,0:T(4,128)(4,1)S(1)} %broadcast_compare_fusion.2, bf16[4,512,2,128]{1,3,2,0:T(8,128)(2,1)} %bitcast.39, bf16[4,2,8,128]{3,2,1,0:T(8,128)(2,1)S(1)} %get-tuple-element.338), kind=kOutput, calls=%fused_computation.5.clone.1 | convolution fusion | flops 8486848 | bytes 1198336 | tf_op jit(solution)/shard_map/while/body/eval_jaxpr/rgjd,rcgd->rgjc/dot_general | solution.py:49
  33.4 1.7 %constant_dynamic-slice_fusion.3 = (bf16[4,512,256]{2,1,0:T(8,128)(2,1)S(1)}, bf16[4,512,256]{2,1,0:T(8,128)(2,1)S(1)}) fusion(bf16[4,4096,256]{2,1,0:T(8,128)(2,1)} %get-tuple-element.339, s32[]{:T(128)S(6)} %select_n.45, bf16[4,4096,256]{2,1,0:T(8,128)(2,1)} %get-tuple-element.337), kind=kLoop, calls=%fused_computation.17.clone.1 | loop fusion | bytes 4194308 | tf_op jit(solution)/shard_map/while/body/eval_jaxpr/dynamic_slice | solution.py:45
  35.1 1.3 %copy.29 = bf16[4,512,256]{1,2,0:T(8,128)(2,1)} copy(bf16[4,512,256]{2,1,0:T(8,128)(2,1)S(1)} %get-tuple-element.300) | data formatting | bytes 2097152 | tf_op jit(solution)/shard_map/while/body/eval_jaxpr/dynamic_slice | solution.py:42
  37.2 1.6 %select_reduce_fusion.2 = (f32[4,2,8]{2,1,0:T(2,128)S(1)}, f32[4,2,512,8]{2,3,1,0:T(8,128)S(1)}) fusion(pred[4,512]{1,0:T(4,128)(4,1)S(1)} %broadcast_compare_fusion.2, bf16[4,512,2,128]{1,3,2,0:T(8,128)(2,1)} %bitcast.39, bf16[4,2,8,128]{3,2,1,0:T(8,128)(2,1)S(1)} %get-tuple-element.338), kind=kOutput, calls=%fused_computation.5.clone.1 | convolution fusion | flops 8486848 | bytes 1198336 | tf_op jit(solution)/shard_map/while/body/eval_jaxpr/rgjd,rcgd->rgjc/dot_general | solution.py:49
  39.9 1.7 %constant_dynamic-slice_fusion.3 = (bf16[4,512,256]{2,1,0:T(8,128)(2,1)S(1)}, bf16[4,512,256]{2,1,0:T(8,128)(2,1)S(1)}) fusion(bf16[4,4096,256]{2,1,0:T(8,128)(2,1)} %get-tuple-element.339, s32[]{:T(128)S(6)} %select_n.45, bf16[4,4096,256]{2,1,0:T(8,128)(2,1)} %get-tuple-element.337), kind=kLoop, calls=%fused_computation.17.clone.1 | loop fusion | bytes 4194308 | tf_op jit(solution)/shard_map/while/body/eval_jaxpr/dynamic_slice | solution.py:45
  41.6 1.3 %copy.29 = bf16[4,512,256]{1,2,0:T(8,128)(2,1)} copy(bf16[4,512,256]{2,1,0:T(8,128)(2,1)S(1)} %get-tuple-element.300) | data formatting | bytes 2097152 | tf_op jit(solution)/shard_map/while/body/eval_jaxpr/dynamic_slice | solution.py:42
  43.7 1.6 %select_reduce_fusion.2 = (f32[4,2,8]{2,1,0:T(2,128)S(1)}, f32[4,2,512,8]{2,3,1,0:T(8,128)S(1)}) fusion(pred[4,512]{1,0:T(4,128)(4,1)S(1)} %broadcast_compare_fusion.2, bf16[4,512,2,128]{1,3,2,0:T(8,128)(2,1)} %bitcast.39, bf16[4,2,8,128]{3,2,1,0:T(8,128)(2,1)S(1)} %get-tuple-element.338), kind=kOutput, calls=%fused_computation.5.clone.1 | convolution fusion | flops 8486848 | bytes 1198336 | tf_op jit(solution)/shard_map/while/body/eval_jaxpr/rgjd,rcgd->rgjc/dot_general | solution.py:49
  46.4 1.7 %constant_dynamic-slice_fusion.3 = (bf16[4,512,256]{2,1,0:T(8,128)(2,1)S(1)}, bf16[4,512,256]{2,1,0:T(8,128)(2,1)S(1)}) fusion(bf16[4,4096,256]{2,1,0:T(8,128)(2,1)} %get-tuple-element.339, s32[]{:T(128)S(6)} %select_n.45, bf16[4,4096,256]{2,1,0:T(8,128)(2,1)} %get-tuple-element.337), kind=kLoop, calls=%fused_computation.17.clone.1 | loop fusion | bytes 4194308 | tf_op jit(solution)/shard_map/while/body/eval_jaxpr/dynamic_slice | solution.py:45
  48.1 1.3 %copy.29 = bf16[4,512,256]{1,2,0:T(8,128)(2,1)} copy(bf16[4,512,256]{2,1,0:T(8,128)(2,1)S(1)} %get-tuple-element.300) | data formatting | bytes 2097152 | tf_op jit(solution)/shard_map/while/body/eval_jaxpr/dynamic_slice | solution.py:42
  50.2 1.6 %select_reduce_fusion.2 = (f32[4,2,8]{2,1,0:T(2,128)S(1)}, f32[4,2,512,8]{2,3,1,0:T(8,128)S(1)}) fusion(pred[4,512]{1,0:T(4,128)(4,1)S(1)} %broadcast_compare_fusion.2, bf16[4,512,2,128]{1,3,2,0:T(8,128)(2,1)} %bitcast.39, bf16[4,2,8,128]{3,2,1,0:T(8,128)(2,1)S(1)} %get-tuple-element.338), kind=kOutput, calls=%fused_computation.5.clone.1 | convolution fusion | flops 8486848 | bytes 1198336 | tf_op jit(solution)/shard_map/while/body/eval_jaxpr/rgjd,rcgd->rgjc/dot_general | solution.py:49
  53.0 1.7 %constant_dynamic-slice_fusion.3 = (bf16[4,512,256]{2,1,0:T(8,128)(2,1)S(1)}, bf16[4,512,256]{2,1,0:T(8,128)(2,1)S(1)}) fusion(bf16[4,4096,256]{2,1,0:T(8,128)(2,1)} %get-tuple-element.339, s32[]{:T(128)S(6)} %select_n.45, bf16[4,4096,256]{2,1,0:T(8,128)(2,1)} %get-tuple-element.337), kind=kLoop, calls=%fused_computation.17.clone.1 | loop fusion | bytes 4194308 | tf_op jit(solution)/shard_map/while/body/eval_jaxpr/dynamic_slice | solution.py:45
  54.7 1.3 %copy.29 = bf16[4,512,256]{1,2,0:T(8,128)(2,1)} copy(bf16[4,512,256]{2,1,0:T(8,128)(2,1)S(1)} %get-tuple-element.300) | data formatting | bytes 2097152 | tf_op jit(solution)/shard_map/while/body/eval_jaxpr/dynamic_slice | solution.py:42
  56.7 1.6 %select_reduce_fusion.2 = (f32[4,2,8]{2,1,0:T(2,128)S(1)}, f32[4,2,512,8]{2,3,1,0:T(8,128)S(1)}) fusion(pred[4,512]{1,0:T(4,128)(4,1)S(1)} %broadcast_compare_fusion.2, bf16[4,512,2,128]{1,3,2,0:T(8,128)(2,1)} %bitcast.39, bf16[4,2,8,128]{3,2,1,0:T(8,128)(2,1)S(1)} %get-tuple-element.338), kind=kOutput, calls=%fused_computation.5.clone.1 | convolution fusion | flops 8486848 | bytes 1198336 | tf_op jit(solution)/shard_map/while/body/eval_jaxpr/rgjd,rcgd->rgjc/dot_general | solution.py:49
  60.1 25.0 %all-gather.1 = f32[128,2,8]{2,1,0:T(2,128)S(1)} all-gather(f32[4,2,8]{2,1,0:T(2,128)S(1)} %get-tuple-element.162), channel_id=3, replica_groups=mesh['ctx'=32,'head'=4] {'ctx'}, dimensions={0}, use_global_device_ids=true | all-gather | bytes 8448 | tf_op jit(solution)/shard_map/all_gather | solution.py:76
  85.2 23.9 %all-gather.2 = f32[128,2,8]{2,1,0:T(2,128)S(1)} all-gather(f32[4,2,8]{2,1,0:T(2,128)S(1)} %get-tuple-element.163), channel_id=4, replica_groups=mesh['ctx'=32,'head'=4] {'ctx'}, dimensions={0}, use_global_device_ids=true | all-gather | bytes 8448 | tf_op jit(solution)/shard_map/all_gather | solution.py:77
  109.4 1.6 %multiply_reduce_fusion = f32[4,2,8,128]{3,2,1,0:T(8,128)S(1)} fusion(f32[32,4,2,8,128]{4,3,2,1,0:T(8,128)} %bitcast.42, f32[32,4,2,8]{3,2,1,0:T(2,128)S(1)} %subtract_exponential_fusion.1), kind=kLoop, calls=%fused_computation.20 | loop fusion | flops 516096 | bytes 1089536 | tf_op jit(solution)/shard_map/reduce_sum | solution.py:22
  111.3 12.3 %psum.7 = f32[4,256]{1,0:T(4,128)} all-reduce(f32[4,256]{1,0:T(4,128)S(1)} %fusion.6), channel_id=1, replica_groups=mesh['ctx'=32,'head'=4] {'head'}, use_global_device_ids=true, to_apply=%region_7.8 | all-reduce | flops 1024 | bytes 8192 | tf_op jit(solution)/shard_map/psum | solution.py:82
  (78 shorter events, 14.9 us)
Async XLA Ops:
  6.5 104.5 %copy-start = (bf16[2048,256]{1,0:T(8,128)(2,1)S(1)}, bf16[2048,256]{1,0:T(8,128)(2,1)}, u32[]{:S(2)}) copy-start(bf16[2048,256]{1,0:T(8,128)(2,1)} %param.11) | copy-start | bytes 3145732
  6.5 102.8 %all-gather.5.cloned.1.call-start = ((), (), s32[]{:S(2)}) async-start(), calls=%async_computation | async-start | bytes 1081344 | tf_op jit(solution)/shard_map/all_gather | solution.py:75
  59.5 0.6 copy-start.1
Sparse Core Ops, SparseCore 0:
  60.2 45.1 all-gather.4
where the time goes:
time: 131 us; the launch traced here: 130 us
  blocking collectives  61.3 us (47%)
  local copies, waits for them, and re-layouts  30 us (23%)
  matrix products  16 us (12%)
  between operations  13.4 us (10%)
  other arithmetic  9.43 us (7%)
    all_gather x1, blocking collectives, on_device(): lax.all_gather(top[None], 'ctx', axis=0, tiled=True)  25 us
    all_gather x1, blocking collectives, on_device(): lax.all_gather(total[None], 'ctx', axis=0, tiled=True)  23.9 us
    dynamic_slice x16, local copies, waits for them, and re-layouts, step(): lax.dynamic_slice_in_dim(cached_value_matrix, index * span, span, 1)  17.8 us
    dot_general x8, matrix products, step(): jnp.einsum('rgjd,rcgd->rgjc', query_rows, key_block, preferred_element_ty...  12.5 us
    psum x1, blocking collectives, on_device(): return lax.psum(partial_value, 'head')  12.3 us
    dynamic_slice x8, local copies, waits for them, and re-layouts, step(): lax.dynamic_slice_in_dim(key_cache, index * span, span, 1)  10.7 us
    lt x8, other arithmetic, step(): valid = (places[None, :] < lengths[:, None])[:, None, None, :]  5.81 us
    dot_general x8, matrix products, step(): jnp.einsum('rgjc,rcgd->rgjd', weights.astype(jnp.bfloat16), value_block,...  3.28 us
  transfers between devices with their start and end apart: 1, of which 0 were waited for; matrix products, arithmetic and copies ran while one was open for 0% of the time, Pallas kernels for 0%

commit v1 on v0

v1 whole, which is shorter than its diff:
```python
import functools

import jax
import jax.numpy as jnp
from jax import lax
from jax.experimental import pallas as pl
from jax.experimental.pallas import tpu as pltpu
from jax.sharding import PartitionSpec as P

HEAD_WIDTH = 128
LOWEST = -1e30
LOG2_E = 1.4426950408889634
PACKED = 72
MIB = 1 << 20


def attention_kernel(rows, heads, ctx_dev, lengths_hbm, query_hbm, key_hbm, value_hbm, out_ref,
                     lengths, query, query_rows, keys, values, scores, weights, small_sem, key_sem, value_sem):
    chunks = key_sem.shape[1]
    span = ctx_dev // chunks
    group = heads // 2

    def key_copy(r, c):
        piece = pl.ds(c * span, span)
        return pltpu.make_async_copy(key_hbm.at[r, piece], keys.at[r, piece], key_sem.at[r, c])

    def value_copy(r, c):
        piece = pl.ds(c * span, span)
        return pltpu.make_async_copy(value_hbm.at[r, piece], values.at[r, piece], value_sem.at[r, c])

    query_copy = pltpu.make_async_copy(query_hbm, query, small_sem.at[0])
    lengths_copy = pltpu.make_async_copy(lengths_hbm, lengths, small_sem.at[1])
    query_copy.start()
    lengths_copy.start()
    for r in range(rows):
        for c in range(chunks):
            key_copy(r, c).start()
    for r in range(rows):
        for c in range(chunks):
            value_copy(r, c).start()
    offset = lax.axis_index("ctx") * ctx_dev
    query_copy.wait()
    lengths_copy.wait()
    wide = query[...].astype(jnp.float32)
    for h in range(heads):
        query_rows[:, h, :] = wide[:, h * HEAD_WIDTH:(h + 1) * HEAD_WIDTH]
    nothing = jnp.zeros((group, HEAD_WIDTH), jnp.float32)
    tops, totals, mixes = [], [], []
    for r in range(rows):
        query_block = jnp.concatenate(
            [
                jnp.concatenate([query_rows[r, :group], nothing], axis=1),
                jnp.concatenate([nothing, query_rows[r, group:]], axis=1),
            ],
            axis=0,
        ).astype(jnp.bfloat16)
        place = offset + lax.broadcasted_iota(jnp.int32, (heads, span), 1)
        top = jnp.full((heads, 1), LOWEST, jnp.float32)
        for c in range(chunks):
            key_copy(r, c).wait()
            score = lax.dot_general(
                query_block, keys[r, c * span:(c + 1) * span], (((1,), (1,)), ((), ())),
                preferred_element_type=jnp.float32,
            ) * jnp.float32(LOG2_E / HEAD_WIDTH**0.5)
            score = jnp.where(place + c * span < lengths[r], score, jnp.float32(LOWEST))
            scores[:, c * span:(c + 1) * span] = score
            top = jnp.maximum(top, jnp.max(score, axis=1, keepdims=True))
        total = jnp.zeros((heads, 1), jnp.float32)
        for c in range(chunks):
            weight = jnp.where(
                place + c * span < lengths[r],
                jnp.exp2(scores[:, c * span:(c + 1) * span] - top),
                jnp.float32(0.0),
            )
            total += jnp.sum(weight, axis=1, keepdims=True)
            weights[r, :, c * span:(c + 1) * span] = weight.astype(jnp.bfloat16)
        tops.append(top)
        totals.append(total)
    for r in range(rows):
        mixed = jnp.zeros((heads, 2 * HEAD_WIDTH), jnp.float32)
        for c in range(chunks):
            value_copy(r, c).wait()
            mixed += jnp.dot(
                weights[r, :, c * span:(c + 1) * span], values[r, c * span:(c + 1) * span],
                preferred_element_type=jnp.float32,
            )
        mixes += [mixed[:group, :HEAD_WIDTH], mixed[group:, HEAD_WIDTH:]]
    lane = lax.broadcasted_iota(jnp.int32, (rows * heads, HEAD_WIDTH), 1)
    stats = jnp.where(lane == 0, jnp.concatenate(tops, axis=0), jnp.concatenate(totals, axis=0))
    turned = jnp.concatenate(mixes + mixes, axis=0).T
    half = rows * heads
    out_ref[:half] = jnp.where(lane < half, turned[:half], turned[half:])
    out_ref[half:] = jnp.concatenate([stats, stats], axis=0).T[:8]


def attention(query, key_cache, value_cache, lengths):
    rows, ctx_dev, kv_cols = key_cache.shape
    heads = query.shape[1] // HEAD_WIDTH
    chunks = 4
    hbm = pl.BlockSpec(memory_space=pl.ANY)
    return pl.pallas_call(
        functools.partial(attention_kernel, rows, heads, ctx_dev),
        out_shape=jax.ShapeDtypeStruct((PACKED, HEAD_WIDTH), jnp.float32),
        in_specs=[hbm] * 4,
        out_specs=pl.BlockSpec(memory_space=pltpu.VMEM),
        scratch_shapes=[
            pltpu.SMEM((rows,), jnp.int32),
            pltpu.VMEM(query.shape, jnp.bfloat16),
            pltpu.VMEM((rows, heads, HEAD_WIDTH), jnp.float32),
            pltpu.VMEM(key_cache.shape, jnp.bfloat16),
            pltpu.VMEM(value_cache.shape, jnp.bfloat16),
            pltpu.VMEM((heads, ctx_dev), jnp.float32),
            pltpu.VMEM((rows, heads, ctx_dev), jnp.bfloat16),
            pltpu.SemaphoreType.DMA((2,)),
            pltpu.SemaphoreType.DMA((rows, chunks)),
            pltpu.SemaphoreType.DMA((rows, chunks)),
        ],
        compiler_params=pltpu.CompilerParams(vmem_limit_bytes=32 * MIB),
        cost_estimate=pl.CostEstimate(
            flops=4 * rows * heads * ctx_dev * kv_cols, bytes_accessed=4 * rows * ctx_dev * kv_cols, transcendentals=0
        ),
    )(lengths, query, key_cache, value_cache)


def merge(pieces):
    half = PACKED - 8
    tops = [p[half:half + 1] for p in pieces]
    top = functools.reduce(jnp.maximum, tops)
    scales = [jnp.exp2(t - top) for t in tops]
    mixed = sum(p[:half] * s for p, s in zip(pieces, scales))
    total = sum(p[half + 1:half + 2] * s for p, s in zip(pieces, scales))
    return mixed, top, total


def merge_kernel(*refs):
    out_ref = refs[-1]
    mixed, top, total = merge([ref[...] for ref in refs[:-1]])
    half = mixed.shape[0]
    out_ref[:half] = mixed
    row = lax.broadcasted_iota(jnp.int32, (8, HEAD_WIDTH), 0)
    out_ref[half:] = jnp.where(row == 0, top, total)


def merge_call(pieces):
    vmem = pl.BlockSpec(memory_space=pltpu.VMEM)
    return pl.pallas_call(
        merge_kernel,
        out_shape=jax.ShapeDtypeStruct((PACKED, HEAD_WIDTH), jnp.float32),
        in_specs=[vmem] * len(pieces),
        out_specs=vmem,
    )(*pieces)


def project_kernel(rows, heads, *refs):
    *pieces, weight_ref, out_ref, attended = refs
    mixed, _, total = merge([ref[...] for ref in pieces])
    mixed = mixed / total
    half = mixed.shape[0]
    attended[...] = jnp.concatenate([mixed, pltpu.roll(mixed, half, 1)], axis=0).T[:half]
    flat = jnp.concatenate([attended[pl.ds(h, rows, stride=heads), :] for h in range(heads)], axis=1)
    out_ref[...] = jnp.dot(flat.astype(jnp.bfloat16), weight_ref[...], preferred_element_type=jnp.float32)


def project_call(pieces, out_weight, rows):
    heads = out_weight.shape[0] // HEAD_WIDTH
    vmem = pl.BlockSpec(memory_space=pltpu.VMEM)
    return pl.pallas_call(
        functools.partial(project_kernel, rows, heads),
        out_shape=jax.ShapeDtypeStruct((rows, out_weight.shape[1]), jnp.float32),
        in_specs=[vmem] * (len(pieces) + 1),
        out_specs=vmem,
        scratch_shapes=[pltpu.VMEM((rows * heads, HEAD_WIDTH), jnp.float32)],
        compiler_params=pltpu.CompilerParams(vmem_limit_bytes=16 * MIB),
    )(*pieces, out_weight)


def exchange(value, axis, bits):
    size = lax.axis_size(axis)
    return [value] + [lax.ppermute(value, axis, [(i, i ^ bit) for i in range(size)]) for bit in bits]


def on_device(query, key_cache, cached_value_matrix, lengths, out_weight):
    rows = query.shape[0]
    packed = attention(query, key_cache, cached_value_matrix, lengths)
    packed = merge_call(exchange(packed, "ctx", (1,)))
    packed = merge_call(exchange(packed, "ctx", (2, 6, 4)))
    partial_value = project_call(exchange(packed, "ctx", (8, 24, 16)), out_weight, rows)
    return functools.reduce(jnp.add, exchange(partial_value, "head", (1, 3, 2)))


def solution(mesh):
    in_specs = (
        P(None, "head"),
        P(None, "ctx", "head"),
        P(None, "ctx", "head"),
        P(),
        P("head", "ctx"),
    )
    out_specs = P(None, "ctx")
    return jax.shard_map(
        on_device, mesh=mesh, in_specs=in_specs, out_specs=out_specs, check_vma=False
    )
```

time: 131 us -> 52.3 us (0.40)
  blocking collectives: 61.3 us -> 0 us
  local copies, waits for them, and re-layouts: 30 us -> 10.7 us
  matrix products: 16 us -> 0 us
  waiting for transfers between devices: 0.04 us -> 13.6 us
  starting transfers between devices: 0.01 us -> 13.5 us
  Pallas kernels: 0 us -> 13.4 us
  between operations: 13.4 us -> 0.05 us
  other arithmetic: 9.43 us -> 0.6 us
    all_gather x2 -> x0, blocking collectives: 48.9 us -> none  [the longest x1 25 us: on_device(): lax.all_gather(top[None], 'ctx', axis=0, tiled=True)]
    dynamic_slice x24 -> x0, local copies, waits for them, and re-layouts: 28.5 us -> none  [the longest x16 17.8 us: step(): lax.dynamic_slice_in_dim(cached_value_matrix, index * span, span, 1)]
    dot_general x17 -> x0, matrix products: 16 us -> none  [the longest x8 12.5 us: step(): jnp.einsum('rgjd,rcgd->rgjc', query_rows, key_block, preferred_element_ty...]
    ppermute x0 -> x10, waiting for transfers between devices: none -> 13.6 us  [exchange(): lax.ppermute(value, axis, [(i, i ^ bit) for i in range(size)])]
    ppermute x0 -> x10, starting transfers between devices: none -> 13.5 us  [exchange(): lax.ppermute(value, axis, [(i, i ^ bit) for i in range(size)])]
    pallas_call x0 -> x4, Pallas kernels: none -> 13.4 us  [the longest x1 10.2 us: attention(): pl.pallas_call(functools.partial(attention_kernel, rows, heads, ctx_dev),...]
    psum x1 -> x0, blocking collectives: 12.3 us -> none  [on_device(): return lax.psum(partial_value, 'head')]
    unnamed x5 -> x22, local copies, waits for them, and re-layouts: 1.42 us -> 10.7 us
  transfers between devices with their start and end apart: 1 -> 10, of which waited for: 0 -> 7; matrix products, arithmetic and copies ran while one was open for 0% -> 0% of each run, Pallas kernels for 0% -> 0%
where the time goes in v1:
time: 52.3 us; the launch traced here: 51.9 us
  waiting for transfers between devices  13.6 us (26%)
  starting transfers between devices  13.5 us (26%)
  Pallas kernels  13.4 us (26%)
  local copies, waits for them, and re-layouts  10.7 us (20%)
  other arithmetic  0.6 us (1%)
    ppermute x10, waiting for transfers between devices, exchange(): lax.ppermute(value, axis, [(i, i ^ bit) for i in range(size)])  13.6 us
    ppermute x10, starting transfers between devices, exchange(): lax.ppermute(value, axis, [(i, i ^ bit) for i in range(size)])  13.5 us
    unnamed x22, local copies, waits for them, and re-layouts  10.7 us
    pallas_call x1, Pallas kernels, attention(): pl.pallas_call(functools.partial(attention_kernel, rows, heads, ctx_dev),...  10.2 us
    pallas_call x2, Pallas kernels, merge_call(): pl.pallas_call(merge_kernel, out_shape=jax.ShapeDtypeStruct((PACKED, HEAD...  2.87 us
  transfers between devices with their start and end apart: 10, of which 7 were waited for; matrix products, arithmetic and copies ran while one was open for 0% of the time, Pallas kernels for 0%

profile of v1, /device:TPU:0, one launch (start us, length us, event | category | flops | bytes accessed | tf_op | source)
XLA Modules:
  0.0 51.9 jit_solution(15777643751762116499)
XLA Ops:
  0.0 3.4 %copy-done = bf16[4,4096,256]{2,1,0:T(8,128)(2,1)S(1)} copy-done((bf16[4,4096,256]{2,1,0:T(8,128)(2,1)S(1)}, bf16[4,4096,256]{2,1,0:T(8,128)(2,1)}, u32[]{:S(2)}) %copy-start) | copy-done | bytes 8388632
  3.4 3.4 %copy-done.1 = bf16[4,4096,256]{2,1,0:T(8,128)(2,1)S(1)} copy-done((bf16[4,4096,256]{2,1,0:T(8,128)(2,1)S(1)}, bf16[4,4096,256]{2,1,0:T(8,128)(2,1)}, u32[]{:S(2)}) %copy-start.1) | copy-done | bytes 8388632
  6.8 0.7 %copy-done.5 = bf16[4,2048]{1,0:T(4,128)(2,1)S(1)} copy-done((bf16[4,2048]{1,0:T(4,128)(2,1)S(1)}, bf16[4,2048]{1,0:T(4,128)(2,1)}, u32[]{:S(2)}) %copy-start.5) | copy-done | bytes 16408
  7.5 0.7 %copy-done.6 = s32[4]{0:T(128)S(1)} copy-done((s32[4]{0:T(128)S(1)}, s32[4]{0:T(128)}, u32[]{:S(2)}) %copy-start.6) | copy-done | bytes 40
  8.1 10.2 %shard_map.55.refs_0_ = f32[72,128]{1,0:T(8,128)S(1)} custom-call(s32[4]{0:T(128)S(1)} %copy-done.6, bf16[4,2048]{1,0:T(4,128)(2,1)S(1)} %copy-done.5, bf16[4,4096,256]{2,1,0:T(8,128)(2,1)S(1)} %copy-done, bf16[4,4096,256]{2,1,0:T(8,128)(2,1)S(1)} %copy-done.1), custom_call_target="tpu_custom_call" | custom-call | flops 268435456 | bytes 16777216 | tf_op jit(solution)/shard_map/pallas_call | solution.py:101
  18.3 0.1 collective-permute-start
  18.4 1.2 %collective-permute-done.refs_1_ = f32[72,128]{1,0:T(8,128)S(1)} collective-permute-done((f32[72,128]{1,0:T(8,128)S(1)}, f32[72,128]{1,0:T(8,128)S(1)}, u32[]{:S(2)}, u32[]{:S(2)}) %collective-permute-start) | collective-permute-done | bytes 36896 | tf_op jit(solution)/shard_map/ppermute | solution.py:179
  19.6 0.6 %copy-done.7 = f32[72,128]{1,0:T(8,128)} copy-done((f32[72,128]{1,0:T(8,128)}, f32[72,128]{1,0:T(8,128)S(1)}, u32[]{:S(2)}) %copy-start.7) | copy-done | bytes 36888
  20.3 1.4 %shard_map.56.refs_0_ = f32[72,128]{1,0:T(8,128)} custom-call(f32[72,128]{1,0:T(8,128)} %copy-done.3, f32[72,128]{1,0:T(8,128)} %copy-done.7), custom_call_target="tpu_custom_call" | custom-call | tf_op jit(solution)/shard_map/pallas_call | solution.py:146
  21.7 3.3 %collective-permute-start.3 = (f32[72,128]{1,0:T(8,128)}, f32[72,128]{1,0:T(8,128)S(1)}, u32[]{:S(2)}, u32[]{:S(2)}) collective-permute-start(f32[72,128]{1,0:T(8,128)} %shard_map.56.refs_0_), channel_id=1, source_target_pairs={{0,16},{4,20},{8,24},{12,28},{16,0},{20,4},{24,8},{28,12},{32,48},... | collective-permute-start | bytes 110600 | tf_op jit(solution)/shard_map/ppermute | solution.py:179
  24.9 1.1 %collective-permute-start.2 = (f32[72,128]{1,0:T(8,128)}, f32[72,128]{1,0:T(8,128)S(1)}, u32[]{:S(2)}, u32[]{:S(2)}) collective-permute-start(f32[72,128]{1,0:T(8,128)} %shard_map.56.refs_0_), channel_id=1, source_target_pairs={{0,24},{4,28},{8,16},{12,20},{16,8},{20,12},{24,0},{28,4},{32,56},... | collective-permute-start | bytes 110600 | tf_op jit(solution)/shard_map/ppermute | solution.py:179
  26.0 0.0 collective-permute-start.1
  26.0 1.3 %collective-permute-done.3.refs_3_ = f32[72,128]{1,0:T(8,128)S(1)} collective-permute-done((f32[72,128]{1,0:T(8,128)}, f32[72,128]{1,0:T(8,128)S(1)}, u32[]{:S(2)}, u32[]{:S(2)}) %collective-permute-start.3) | collective-permute-done | bytes 36896 | tf_op jit(solution)/shard_map/ppermute | solution.py:179
  27.3 3.0 %collective-permute-done.2.refs_2_ = f32[72,128]{1,0:T(8,128)S(1)} collective-permute-done((f32[72,128]{1,0:T(8,128)}, f32[72,128]{1,0:T(8,128)S(1)}, u32[]{:S(2)}, u32[]{:S(2)}) %collective-permute-start.2) | collective-permute-done | bytes 36896 | tf_op jit(solution)/shard_map/ppermute | solution.py:179
  30.3 0.0 collective-permute-done.1.refs_1_
  30.3 0.6 %copy-done.9 = f32[72,128]{1,0:T(8,128)} copy-done((f32[72,128]{1,0:T(8,128)}, f32[72,128]{1,0:T(8,128)S(1)}, u32[]{:S(2)}) %copy-start.9) | copy-done | bytes 36888
  30.9 0.6 %copy-done.10 = f32[72,128]{1,0:T(8,128)} copy-done((f32[72,128]{1,0:T(8,128)}, f32[72,128]{1,0:T(8,128)S(1)}, u32[]{:S(2)}) %copy-start.10) | copy-done | bytes 36888
  31.5 1.5 %shard_map.57.refs_0_ = f32[72,128]{1,0:T(8,128)} custom-call(f32[72,128]{1,0:T(8,128)} %shard_map.56.refs_0_, f32[72,128]{1,0:T(8,128)} %copy-done.10, f32[72,128]{1,0:T(8,128)} %copy-done.9, f32[72,128]{1,0:T(8,128)} %copy-done.8), custom_call_target="tpu_custom_call" | custom-call | tf_op jit(solution)/shard_map/pallas_call | solution.py:146
  33.0 3.0 %collective-permute-start.6 = (f32[72,128]{1,0:T(8,128)}, f32[72,128]{1,0:T(8,128)S(1)}, u32[]{:S(2)}, u32[]{:S(2)}) collective-permute-start(f32[72,128]{1,0:T(8,128)} %shard_map.57.refs_0_), channel_id=1, source_target_pairs={{0,64},{4,68},{8,72},{12,76},{16,80},{20,84},{24,88},{28,92},{32,9... | collective-permute-start | bytes 110600 | tf_op jit(solution)/shard_map/ppermute | solution.py:179
  36.0 1.1 %collective-permute-start.5 = (f32[72,128]{1,0:T(8,128)}, f32[72,128]{1,0:T(8,128)S(1)}, u32[]{:S(2)}, u32[]{:S(2)}) collective-permute-start(f32[72,128]{1,0:T(8,128)} %shard_map.57.refs_0_), channel_id=1, source_target_pairs={{0,96},{4,100},{8,104},{12,108},{16,112},{20,116},{24,120},{28,124... | collective-permute-start | bytes 110600 | tf_op jit(solution)/shard_map/ppermute | solution.py:179
  37.2 0.0 collective-permute-start.4
  37.2 1.5 %collective-permute-done.6.refs_3_ = f32[72,128]{1,0:T(8,128)S(1)} collective-permute-done((f32[72,128]{1,0:T(8,128)}, f32[72,128]{1,0:T(8,128)S(1)}, u32[]{:S(2)}, u32[]{:S(2)}) %collective-permute-start.6) | collective-permute-done | bytes 36896 | tf_op jit(solution)/shard_map/ppermute | solution.py:179
  38.7 2.7 %collective-permute-done.5.refs_2_ = f32[72,128]{1,0:T(8,128)S(1)} collective-permute-done((f32[72,128]{1,0:T(8,128)}, f32[72,128]{1,0:T(8,128)S(1)}, u32[]{:S(2)}, u32[]{:S(2)}) %collective-permute-start.5) | collective-permute-done | bytes 36896 | tf_op jit(solution)/shard_map/ppermute | solution.py:179
  41.4 0.0 collective-permute-done.4.refs_1_
  41.4 0.8 %copy-done.4 = f32[72,128]{1,0:T(8,128)S(1)} copy-done((f32[72,128]{1,0:T(8,128)S(1)}, f32[72,128]{1,0:T(8,128)}, u32[]{:S(2)}) %copy-start.4) | copy-done | bytes 36888
  42.2 0.4 shard_map.58
  42.6 3.9 %collective-permute-start.9 = (f32[4,256]{1,0:T(4,128)S(1)}, f32[4,256]{1,0:T(4,128)S(1)}, u32[]{:S(2)}, u32[]{:S(2)}) collective-permute-start(f32[4,256]{1,0:T(4,128)S(1)} %shard_map.58), channel_id=1, source_target_pairs={{0,2},{1,3},{2,0},{3,1},{4,6},{5,7},{6,4},{7,5},{8,10},{9,11},{10,... | collective-permute-start | bytes 12296 | tf_op jit(solution)/shard_map/ppermute | solution.py:179
  46.4 0.7 %collective-permute-start.8 = (f32[4,256]{1,0:T(4,128)S(1)}, f32[4,256]{1,0:T(4,128)S(1)}, u32[]{:S(2)}, u32[]{:S(2)}) collective-permute-start(f32[4,256]{1,0:T(4,128)S(1)} %shard_map.58), channel_id=1, source_target_pairs={{0,3},{1,2},{2,1},{3,0},{4,7},{5,6},{6,5},{7,4},{8,11},{9,10},{10,... | collective-permute-start | bytes 12296 | tf_op jit(solution)/shard_map/ppermute | solution.py:179
  47.2 0.3 collective-permute-start.7
  47.5 0.6 %collective-permute-done.9 = f32[4,256]{1,0:T(4,128)S(1)} collective-permute-done((f32[4,256]{1,0:T(4,128)S(1)}, f32[4,256]{1,0:T(4,128)S(1)}, u32[]{:S(2)}, u32[]{:S(2)}) %collective-permute-start.9) | collective-permute-done | bytes 4128 | tf_op jit(solution)/shard_map/ppermute | solution.py:179
  48.0 3.2 %collective-permute-done.8 = f32[4,256]{1,0:T(4,128)S(1)} collective-permute-done((f32[4,256]{1,0:T(4,128)S(1)}, f32[4,256]{1,0:T(4,128)S(1)}, u32[]{:S(2)}, u32[]{:S(2)}) %collective-permute-start.8) | collective-permute-done | bytes 4128 | tf_op jit(solution)/shard_map/ppermute | solution.py:179
  51.3 0.6 %add_add_fusion = f32[4,256]{1,0:T(4,128)} fusion(f32[4,256]{1,0:T(4,128)S(1)} %collective-permute-done.9, f32[4,256]{1,0:T(4,128)S(1)} %collective-permute-done.8, f32[4,256]{1,0:T(4,128)S(1)} %shard_map.58, f32[4,256]{1,0:T(4,128)S(1)} %collective-permute-done.7), kind=kLoop, calls=%fused_computation | loop fusion | flops 3072 | bytes 20480 | tf_op jit(solution)/shard_map/add | solution.py:188
  (15 shorter events, 0.0 us)
Async XLA Ops:
  0.0 3.4 %copy-start = (bf16[4,4096,256]{2,1,0:T(8,128)(2,1)S(1)}, bf16[4,4096,256]{2,1,0:T(8,128)(2,1)}, u32[]{:S(2)}) copy-start(bf16[4,4096,256]{2,1,0:T(8,128)(2,1)} %key_hbm.1) | copy-start | bytes 25165828
  3.4 3.4 %copy-start.1 = (bf16[4,4096,256]{2,1,0:T(8,128)(2,1)S(1)}, bf16[4,4096,256]{2,1,0:T(8,128)(2,1)}, u32[]{:S(2)}) copy-start(bf16[4,4096,256]{2,1,0:T(8,128)(2,1)} %value_hbm.1) | copy-start | bytes 25165828
  6.8 0.7 %copy-start.5 = (bf16[4,2048]{1,0:T(4,128)(2,1)S(1)}, bf16[4,2048]{1,0:T(4,128)(2,1)}, u32[]{:S(2)}) copy-start(bf16[4,2048]{1,0:T(4,128)(2,1)} %query_hbm.1) | copy-start | bytes 49156
  7.5 0.7 %copy-start.6 = (s32[4]{0:T(128)S(1)}, s32[4]{0:T(128)}, u32[]{:S(2)}) copy-start(s32[4]{0:T(128)} %lengths_hbm.1) | copy-start | bytes 52
  8.1 33.3 %copy-start.2 = (bf16[2048,256]{1,0:T(8,128)(2,1)S(1)}, bf16[2048,256]{1,0:T(8,128)(2,1)}, u32[]{:S(2)}) copy-start(bf16[2048,256]{1,0:T(8,128)(2,1)} %refs_4_.1) | copy-start | bytes 3145732
  18.3 1.3 %copy-start.3 = (f32[72,128]{1,0:T(8,128)}, f32[72,128]{1,0:T(8,128)S(1)}, u32[]{:S(2)}) copy-start(f32[72,128]{1,0:T(8,128)S(1)} %shard_map.55.refs_0_) | copy-start | bytes 110596
  18.3 1.3 %collective-permute-start = (f32[72,128]{1,0:T(8,128)S(1)}, f32[72,128]{1,0:T(8,128)S(1)}, u32[]{:S(2)}, u32[]{:S(2)}) collective-permute-start(f32[72,128]{1,0:T(8,128)S(1)} %shard_map.55.refs_0_), channel_id=1, source_target_pairs={{0,4},{4,0},{8,12},{12,8},{16,20},{20,16},{24,28},{28,24},{32,36},... | collective-permute-start | bytes 110600 | tf_op jit(solution)/shard_map/ppermute | solution.py:179
  19.6 0.6 %copy-start.7 = (f32[72,128]{1,0:T(8,128)}, f32[72,128]{1,0:T(8,128)S(1)}, u32[]{:S(2)}) copy-start(f32[72,128]{1,0:T(8,128)S(1)} %collective-permute-done.refs_1_) | copy-start | bytes 110596
  21.7 5.7 %collective-permute-start.3 = (f32[72,128]{1,0:T(8,128)}, f32[72,128]{1,0:T(8,128)S(1)}, u32[]{:S(2)}, u32[]{:S(2)}) collective-permute-start(f32[72,128]{1,0:T(8,128)} %shard_map.56.refs_0_), channel_id=1, source_target_pairs={{0,16},{4,20},{8,24},{12,28},{16,0},{20,4},{24,8},{28,12},{32,48},... | collective-permute-start | bytes 110600 | tf_op jit(solution)/shard_map/ppermute | solution.py:179
  24.9 5.4 %collective-permute-start.2 = (f32[72,128]{1,0:T(8,128)}, f32[72,128]{1,0:T(8,128)S(1)}, u32[]{:S(2)}, u32[]{:S(2)}) collective-permute-start(f32[72,128]{1,0:T(8,128)} %shard_map.56.refs_0_), channel_id=1, source_target_pairs={{0,24},{4,28},{8,16},{12,20},{16,8},{20,12},{24,0},{28,4},{32,56},... | collective-permute-start | bytes 110600 | tf_op jit(solution)/shard_map/ppermute | solution.py:179
  26.0 4.3 %collective-permute-start.1 = (f32[72,128]{1,0:T(8,128)}, f32[72,128]{1,0:T(8,128)S(1)}, u32[]{:S(2)}, u32[]{:S(2)}) collective-permute-start(f32[72,128]{1,0:T(8,128)} %shard_map.56.refs_0_), channel_id=1, source_target_pairs={{0,8},{4,12},{8,0},{12,4},{16,24},{20,28},{24,16},{28,20},{32,40},... | collective-permute-start | bytes 110600 | tf_op jit(solution)/shard_map/ppermute | solution.py:179
  27.3 3.0 %copy-start.8 = (f32[72,128]{1,0:T(8,128)}, f32[72,128]{1,0:T(8,128)S(1)}, u32[]{:S(2)}) copy-start(f32[72,128]{1,0:T(8,128)S(1)} %collective-permute-done.3.refs_3_) | copy-start | bytes 110596
  30.3 0.6 %copy-start.9 = (f32[72,128]{1,0:T(8,128)}, f32[72,128]{1,0:T(8,128)S(1)}, u32[]{:S(2)}) copy-start(f32[72,128]{1,0:T(8,128)S(1)} %collective-permute-done.2.refs_2_) | copy-start | bytes 110596
  30.9 0.6 %copy-start.10 = (f32[72,128]{1,0:T(8,128)}, f32[72,128]{1,0:T(8,128)S(1)}, u32[]{:S(2)}) copy-start(f32[72,128]{1,0:T(8,128)S(1)} %collective-permute-done.1.refs_1_) | copy-start | bytes 110596
  33.0 5.7 %collective-permute-start.6 = (f32[72,128]{1,0:T(8,128)}, f32[72,128]{1,0:T(8,128)S(1)}, u32[]{:S(2)}, u32[]{:S(2)}) collective-permute-start(f32[72,128]{1,0:T(8,128)} %shard_map.57.refs_0_), channel_id=1, source_target_pairs={{0,64},{4,68},{8,72},{12,76},{16,80},{20,84},{24,88},{28,92},{32,9... | collective-permute-start | bytes 110600 | tf_op jit(solution)/shard_map/ppermute | solution.py:179
  36.0 5.4 %collective-permute-start.5 = (f32[72,128]{1,0:T(8,128)}, f32[72,128]{1,0:T(8,128)S(1)}, u32[]{:S(2)}, u32[]{:S(2)}) collective-permute-start(f32[72,128]{1,0:T(8,128)} %shard_map.57.refs_0_), channel_id=1, source_target_pairs={{0,96},{4,100},{8,104},{12,108},{16,112},{20,116},{24,120},{28,124... | collective-permute-start | bytes 110600 | tf_op jit(solution)/shard_map/ppermute | solution.py:179
  37.2 4.2 %collective-permute-start.4 = (f32[72,128]{1,0:T(8,128)}, f32[72,128]{1,0:T(8,128)S(1)}, u32[]{:S(2)}, u32[]{:S(2)}) collective-permute-start(f32[72,128]{1,0:T(8,128)} %shard_map.57.refs_0_), channel_id=1, source_target_pairs={{0,32},{4,36},{8,40},{12,44},{16,48},{20,52},{24,56},{28,60},{32,0... | collective-permute-start | bytes 110600 | tf_op jit(solution)/shard_map/ppermute | solution.py:179
  41.4 0.8 %copy-start.4 = (f32[72,128]{1,0:T(8,128)S(1)}, f32[72,128]{1,0:T(8,128)}, u32[]{:S(2)}) copy-start(f32[72,128]{1,0:T(8,128)} %shard_map.57.refs_0_) | copy-start | bytes 110596
  42.6 5.5 %collective-permute-start.9 = (f32[4,256]{1,0:T(4,128)S(1)}, f32[4,256]{1,0:T(4,128)S(1)}, u32[]{:S(2)}, u32[]{:S(2)}) collective-permute-start(f32[4,256]{1,0:T(4,128)S(1)} %shard_map.58), channel_id=1, source_target_pairs={{0,2},{1,3},{2,0},{3,1},{4,6},{5,7},{6,4},{7,5},{8,10},{9,11},{10,... | collective-permute-start | bytes 12296 | tf_op jit(solution)/shard_map/ppermute | solution.py:179
  46.4 4.8 %collective-permute-start.8 = (f32[4,256]{1,0:T(4,128)S(1)}, f32[4,256]{1,0:T(4,128)S(1)}, u32[]{:S(2)}, u32[]{:S(2)}) collective-permute-start(f32[4,256]{1,0:T(4,128)S(1)} %shard_map.58), channel_id=1, source_target_pairs={{0,3},{1,2},{2,1},{3,0},{4,7},{5,6},{6,5},{7,4},{8,11},{9,10},{10,... | collective-permute-start | bytes 12296 | tf_op jit(solution)/shard_map/ppermute | solution.py:179
  47.2 4.1 %collective-permute-start.7 = (f32[4,256]{1,0:T(4,128)S(1)}, f32[4,256]{1,0:T(4,128)S(1)}, u32[]{:S(2)}, u32[]{:S(2)}) collective-permute-start(f32[4,256]{1,0:T(4,128)S(1)} %shard_map.58), channel_id=1, source_target_pairs={{0,1},{1,0},{2,3},{3,2},{4,5},{5,4},{6,7},{7,6},{8,9},{9,8},{10,11... | collective-permute-start | bytes 12296 | tf_op jit(solution)/shard_map/ppermute | solution.py:179

commit v2 on v1

v2 whole, which is shorter than its diff:
```python
import functools

import jax
import jax.numpy as jnp
from jax import lax
from jax.experimental import pallas as pl
from jax.experimental.pallas import tpu as pltpu
from jax.sharding import PartitionSpec as P

HEAD_WIDTH = 128
LOWEST = -1e30
LOG2_E = 1.4426950408889634
PACKED = 72
MIB = 1 << 20


def attention_kernel(per, ahead, lengths_hbm, query_hbm, key_hbm, value_hbm, out_ref,
                     lengths, query, query_rows, keys, values, scores, weights, small_sem, key_sem, value_sem):
    rows, ctx_dev, _ = keys.shape
    heads = query_rows.shape[1]
    group = heads // 2
    span = ctx_dev // per
    units = rows * per
    lag = 2

    def copy(unit, source, target, sem):
        r, c = divmod(unit, per)
        piece = pl.ds(c * span, span)
        return pltpu.make_async_copy(source.at[r, piece], target.at[r, piece], sem.at[unit])

    needs = [[] for _ in range(units + lag)]
    for unit in range(units):
        needs[unit].append(copy(unit, key_hbm, keys, key_sem))
        needs[unit + lag].append(copy(unit, value_hbm, values, value_sem))
    queue = [c for step in needs for c in step]
    query_copy = pltpu.make_async_copy(query_hbm, query, small_sem.at[0])
    lengths_copy = pltpu.make_async_copy(lengths_hbm, lengths, small_sem.at[1])
    query_copy.start()
    lengths_copy.start()
    for c in queue[:ahead]:
        c.start()
    started = min(ahead, len(queue))
    waited = 0

    offset = lax.axis_index("ctx") * ctx_dev
    query_copy.wait()
    lengths_copy.wait()
    wide = query[...].astype(jnp.float32)
    for h in range(heads):
        query_rows[:, h, :] = wide[:, h * HEAD_WIDTH:(h + 1) * HEAD_WIDTH]
    nothing = jnp.zeros((group, HEAD_WIDTH), jnp.float32)
    place = lax.broadcasted_iota(jnp.int32, (heads, span), 1)
    blocks, tops, totals, mixes = [], [], [], []
    for r in range(rows):
        blocks.append(
            jnp.concatenate(
                [
                    jnp.concatenate([query_rows[r, :group], nothing], axis=1),
                    jnp.concatenate([nothing, query_rows[r, group:]], axis=1),
                ],
                axis=0,
            ).astype(jnp.bfloat16)
        )
    for step in range(units + lag):
        for c in needs[step]:
            c.wait()
        waited += len(needs[step])
        for c in queue[started:waited + ahead]:
            c.start()
        started = max(started, min(waited + ahead, len(queue)))
        if step < units:
            r, c = divmod(step, per)
            scores[step % 2] = lax.dot_general(
                blocks[r], keys[r, c * span:(c + 1) * span], (((1,), (1,)), ((), ())),
                preferred_element_type=jnp.float32,
            )
        if 1 <= step <= units:
            r, c = divmod(step - 1, per)
            valid = place < lengths[r] - offset - c * span
            score = jnp.where(
                valid, scores[(step - 1) % 2] * jnp.float32(LOG2_E / HEAD_WIDTH**0.5), jnp.float32(LOWEST)
            )
            top = jnp.max(score, axis=1, keepdims=True)
            weight = jnp.where(valid, jnp.exp2(score - top), jnp.float32(0.0))
            tops.append(top)
            totals.append(jnp.sum(weight, axis=1, keepdims=True))
            weights[(step - 1) % 2] = weight.astype(jnp.bfloat16)
        if step >= lag:
            r, c = divmod(step - lag, per)
            both = jnp.dot(
                weights[step % 2], values[r, c * span:(c + 1) * span], preferred_element_type=jnp.float32
            )
            mixes.append(jnp.concatenate([both[:group, :HEAD_WIDTH], both[group:, HEAD_WIDTH:]], axis=0))
    row_mixes, row_tops, row_totals = [], [], []
    for r in range(rows):
        mine = slice(r * per, (r + 1) * per)
        top = functools.reduce(jnp.maximum, tops[mine])
        scales = [jnp.exp2(t - top) for t in tops[mine]]
        row_tops.append(top)
        row_totals.append(sum(t * s for t, s in zip(totals[mine], scales)))
        row_mixes.append(sum(m * s for m, s in zip(mixes[mine], scales)))
    lane = lax.broadcasted_iota(jnp.int32, (rows * heads, HEAD_WIDTH), 1)
    stats = jnp.where(lane == 0, jnp.concatenate(row_tops, axis=0), jnp.concatenate(row_totals, axis=0))
    turned = jnp.concatenate(row_mixes + row_mixes, axis=0).T
    half = rows * heads
    out_ref[:half] = jnp.where(lane < half, turned[:half], turned[half:])
    out_ref[half:] = jnp.concatenate([stats, stats], axis=0).T[:8]


def attention(query, key_cache, value_cache, lengths):
    rows, ctx_dev, kv_cols = key_cache.shape
    heads = query.shape[1] // HEAD_WIDTH
    per, ahead = 2, 8
    span = ctx_dev // per
    hbm = pl.BlockSpec(memory_space=pltpu.HBM)
    vmem = pl.BlockSpec(memory_space=pltpu.VMEM)
    return pl.pallas_call(
        functools.partial(attention_kernel, per, ahead),
        out_shape=jax.ShapeDtypeStruct((PACKED, HEAD_WIDTH), jnp.float32),
        in_specs=[hbm] * 4,
        out_specs=vmem,
        scratch_shapes=[
            pltpu.SMEM((rows,), jnp.int32),
            pltpu.VMEM(query.shape, jnp.bfloat16),
            pltpu.VMEM((rows, heads, HEAD_WIDTH), jnp.float32),
            pltpu.VMEM(key_cache.shape, jnp.bfloat16),
            pltpu.VMEM(value_cache.shape, jnp.bfloat16),
            pltpu.VMEM((2, heads, span), jnp.float32),
            pltpu.VMEM((2, heads, span), jnp.bfloat16),
            pltpu.SemaphoreType.DMA((2,)),
            pltpu.SemaphoreType.DMA((rows * per,)),
            pltpu.SemaphoreType.DMA((rows * per,)),
        ],
        compiler_params=pltpu.CompilerParams(vmem_limit_bytes=54 * MIB),
        cost_estimate=pl.CostEstimate(
            flops=4 * rows * heads * ctx_dev * kv_cols, bytes_accessed=4 * rows * ctx_dev * kv_cols, transcendentals=0
        ),
    )(lengths, query, key_cache, value_cache)


def fetch_kernel(source, target, sem):
    copy = pltpu.make_async_copy(source, target, sem)
    copy.start()
    copy.wait()


def fetch(packed):
    return pl.pallas_call(
        fetch_kernel,
        out_shape=jax.ShapeDtypeStruct(packed.shape, packed.dtype),
        in_specs=[pl.BlockSpec(memory_space=pltpu.HBM)],
        out_specs=pl.BlockSpec(memory_space=pltpu.VMEM),
        scratch_shapes=[pltpu.SemaphoreType.DMA],
        compiler_params=pltpu.CompilerParams(vmem_limit_bytes=4 * MIB),
        cost_estimate=pl.CostEstimate(flops=0, bytes_accessed=packed.size * 4, transcendentals=0),
    )(packed)


def merge(pieces):
    half = PACKED - 8
    tops = [p[half:half + 1] for p in pieces]
    top = functools.reduce(jnp.maximum, tops)
    scales = [jnp.exp2(t - top) for t in tops]
    mixed = sum(p[:half] * s for p, s in zip(pieces, scales))
    total = sum(p[half + 1:half + 2] * s for p, s in zip(pieces, scales))
    return mixed, top, total


def merge_kernel(*refs):
    out_ref = refs[-1]
    mixed, top, total = merge([ref[...] for ref in refs[:-1]])
    half = mixed.shape[0]
    out_ref[:half] = mixed
    row = lax.broadcasted_iota(jnp.int32, (8, HEAD_WIDTH), 0)
    out_ref[half:] = jnp.where(row == 0, top, total)


def merge_call(pieces):
    vmem = pl.BlockSpec(memory_space=pltpu.VMEM)
    return pl.pallas_call(
        merge_kernel,
        out_shape=jax.ShapeDtypeStruct((PACKED, HEAD_WIDTH), jnp.float32),
        in_specs=[vmem] * len(pieces),
        out_specs=vmem,
        compiler_params=pltpu.CompilerParams(vmem_limit_bytes=4 * MIB),
    )(*pieces)


def project_kernel(rows, heads, *refs):
    *pieces, weight_ref, out_ref, attended = refs
    mixed, _, total = merge([ref[...] for ref in pieces])
    mixed = mixed / total
    half = mixed.shape[0]
    attended[...] = jnp.concatenate([mixed, pltpu.roll(mixed, half, 1)], axis=0).T[:half]
    flat = jnp.concatenate([attended[pl.ds(h, rows, stride=heads), :] for h in range(heads)], axis=1)
    out_ref[...] = jnp.dot(flat.astype(jnp.bfloat16), weight_ref[...], preferred_element_type=jnp.float32)


def project_call(pieces, out_weight, rows):
    heads = out_weight.shape[0] // HEAD_WIDTH
    vmem = pl.BlockSpec(memory_space=pltpu.VMEM)
    return pl.pallas_call(
        functools.partial(project_kernel, rows, heads),
        out_shape=jax.ShapeDtypeStruct((rows, out_weight.shape[1]), jnp.float32),
        in_specs=[vmem] * (len(pieces) + 1),
        out_specs=vmem,
        scratch_shapes=[pltpu.VMEM((rows * heads, HEAD_WIDTH), jnp.float32)],
        compiler_params=pltpu.CompilerParams(vmem_limit_bytes=16 * MIB),
    )(*pieces, out_weight)


def exchange(value, axis, bits):
    size = lax.axis_size(axis)
    return [value] + [lax.ppermute(value, axis, [(i, i ^ bit) for i in range(size)]) for bit in bits]


def on_device(query, key_cache, cached_value_matrix, lengths, out_weight):
    rows = query.shape[0]
    packed = attention(query, key_cache, cached_value_matrix, lengths)
    packed = merge_call([fetch(packed)] + exchange(packed, "ctx", (1,))[1:])
    packed = merge_call(exchange(packed, "ctx", (2, 6, 4)))
    partial_value = project_call(exchange(packed, "ctx", (8, 24, 16)), out_weight, rows)
    return functools.reduce(jnp.add, exchange(partial_value, "head", (1, 3, 2)))


def solution(mesh):
    in_specs = (
        P(None, "head"),
        P(None, "ctx", "head"),
        P(None, "ctx", "head"),
        P(),
        P("head", "ctx"),
    )
    out_specs = P(None, "ctx")
    return jax.shard_map(
        on_device, mesh=mesh, in_specs=in_specs, out_specs=out_specs, check_vma=False
    )
```

time: 52.3 us -> 36.2 us (0.69)
  local copies, waits for them, and re-layouts: 10.7 us -> 0.76 us
  Pallas kernels: 13.4 us -> 8.38 us
  waiting for transfers between devices: 13.6 us -> 12.6 us
    unnamed x22 -> x4, local copies, waits for them, and re-layouts: 10.7 us -> 0.76 us
    pallas_call x2, Pallas kernels: 2.87 us -> 0.04 us  [merge_call(): pl.pallas_call(merge_kernel, out_shape=jax.ShapeDtypeStruct((PACKED, HEAD...]
    pallas_call x1 -> x2, Pallas kernels: 10.2 us -> 7.96 us  [the longest x1 7.94 us: attention(): pl.pallas_call(functools.partial(attention_kernel, per, ahead), out_shape...]
    ppermute x10, waiting for transfers between devices: 13.6 us -> 12.6 us  [exchange(): lax.ppermute(value, axis, [(i, i ^ bit) for i in range(size)])]
where the time goes in v2:
time: 36.2 us; the launch traced here: 36 us
  starting transfers between devices  13.7 us (38%)
  waiting for transfers between devices  12.6 us (35%)
  Pallas kernels  8.38 us (23%)
  local copies, waits for them, and re-layouts  0.76 us (2%)
  other arithmetic  0.6 us (2%)
    ppermute x10, starting transfers between devices, exchange(): lax.ppermute(value, axis, [(i, i ^ bit) for i in range(size)])  13.7 us
    ppermute x10, waiting for transfers between devices, exchange(): lax.ppermute(value, axis, [(i, i ^ bit) for i in range(size)])  12.6 us
    pallas_call x1, Pallas kernels, attention(): pl.pallas_call(functools.partial(attention_kernel, per, ahead), out_shape...  7.94 us
    unnamed x4, local copies, waits for them, and re-layouts  0.76 us
  transfers between devices with their start and end apart: 10, of which 7 were waited for; matrix products, arithmetic and copies ran while one was open for 0% of the time, Pallas kernels for 0%

profile of v2, /device:TPU:0, one launch (start us, length us, event | category | flops | bytes accessed | tf_op | source)
XLA Modules:
  0.0 36.0 jit_solution(15785919847753577970)
XLA Ops:
  0.0 0.0 copy-start
  0.0 7.9 %shard_map.55.source = f32[72,128]{1,0:T(8,128)} custom-call(s32[4]{0:T(128)} %lengths_hbm.1, bf16[4,2048]{1,0:T(4,128)(2,1)} %query_hbm.1, bf16[4,4096,256]{2,1,0:T(8,128)(2,1)} %key_hbm.1, bf16[4,4096,256]{2,1,0:T(8,128)(2,1)} %value_hbm.1), custom_call_target="tpu_custom_call" | custom-call | flops 268435456 | bytes 16777216 | tf_op jit(solution)/shard_map/pallas_call | solution.py:117
  7.9 0.1 collective-permute-start
  8.0 0.0 copy-start.1
  8.1 0.8 %copy-done.1 = f32[72,128]{1,0:T(8,128)S(1)} copy-done((f32[72,128]{1,0:T(8,128)S(1)}, f32[72,128]{1,0:T(8,128)}, u32[]{:S(2)}) %copy-start.1) | copy-done | bytes 36888
  8.8 0.6 %collective-permute-done.refs_1_ = f32[72,128]{1,0:T(8,128)S(1)} collective-permute-done((f32[72,128]{1,0:T(8,128)}, f32[72,128]{1,0:T(8,128)S(1)}, u32[]{:S(2)}, u32[]{:S(2)}) %collective-permute-start) | collective-permute-done | bytes 36896 | tf_op jit(solution)/shard_map/ppermute | solution.py:214
  9.5 3.4 %collective-permute-start.3 = (f32[72,128]{1,0:T(8,128)S(1)}, f32[72,128]{1,0:T(8,128)S(1)}, u32[]{:S(2)}, u32[]{:S(2)}) collective-permute-start(f32[72,128]{1,0:T(8,128)S(1)} %shard_map.57.refs_0_), channel_id=1, source_target_pairs={{0,16},{4,20},{8,24},{12,28},{16,0},{20,4},{24,8},{28,12},{32,48},... | collective-permute-start | bytes 110600 | tf_op jit(solution)/shard_map/ppermute | solution.py:214
  12.8 1.1 %collective-permute-start.2 = (f32[72,128]{1,0:T(8,128)S(1)}, f32[72,128]{1,0:T(8,128)S(1)}, u32[]{:S(2)}, u32[]{:S(2)}) collective-permute-start(f32[72,128]{1,0:T(8,128)S(1)} %shard_map.57.refs_0_), channel_id=1, source_target_pairs={{0,24},{4,28},{8,16},{12,20},{16,8},{20,12},{24,0},{28,4},{32,56},... | collective-permute-start | bytes 110600 | tf_op jit(solution)/shard_map/ppermute | solution.py:214
  13.9 0.0 collective-permute-start.1
  13.9 1.1 %collective-permute-done.3.refs_3_ = f32[72,128]{1,0:T(8,128)S(1)} collective-permute-done((f32[72,128]{1,0:T(8,128)S(1)}, f32[72,128]{1,0:T(8,128)S(1)}, u32[]{:S(2)}, u32[]{:S(2)}) %collective-permute-start.3) | collective-permute-done | bytes 36896 | tf_op jit(solution)/shard_map/ppermute | solution.py:214
  15.0 3.0 %collective-permute-done.2.refs_2_ = f32[72,128]{1,0:T(8,128)S(1)} collective-permute-done((f32[72,128]{1,0:T(8,128)S(1)}, f32[72,128]{1,0:T(8,128)S(1)}, u32[]{:S(2)}, u32[]{:S(2)}) %collective-permute-start.2) | collective-permute-done | bytes 36896 | tf_op jit(solution)/shard_map/ppermute | solution.py:214
  18.0 0.0 collective-permute-done.1.refs_1_
  18.0 3.1 %collective-permute-start.6 = (f32[72,128]{1,0:T(8,128)S(1)}, f32[72,128]{1,0:T(8,128)S(1)}, u32[]{:S(2)}, u32[]{:S(2)}) collective-permute-start(f32[72,128]{1,0:T(8,128)S(1)} %shard_map.58.refs_0_), channel_id=1, source_target_pairs={{0,64},{4,68},{8,72},{12,76},{16,80},{20,84},{24,88},{28,92},{32,9... | collective-permute-start | bytes 110600 | tf_op jit(solution)/shard_map/ppermute | solution.py:214
  21.1 1.1 %collective-permute-start.5 = (f32[72,128]{1,0:T(8,128)S(1)}, f32[72,128]{1,0:T(8,128)S(1)}, u32[]{:S(2)}, u32[]{:S(2)}) collective-permute-start(f32[72,128]{1,0:T(8,128)S(1)} %shard_map.58.refs_0_), channel_id=1, source_target_pairs={{0,96},{4,100},{8,104},{12,108},{16,112},{20,116},{24,120},{28,124... | collective-permute-start | bytes 110600 | tf_op jit(solution)/shard_map/ppermute | solution.py:214
  22.3 0.0 collective-permute-start.4
  22.3 1.3 %collective-permute-done.6.refs_3_ = f32[72,128]{1,0:T(8,128)S(1)} collective-permute-done((f32[72,128]{1,0:T(8,128)S(1)}, f32[72,128]{1,0:T(8,128)S(1)}, u32[]{:S(2)}, u32[]{:S(2)}) %collective-permute-start.6) | collective-permute-done | bytes 36896 | tf_op jit(solution)/shard_map/ppermute | solution.py:214
  23.6 2.7 %collective-permute-done.5.refs_2_ = f32[72,128]{1,0:T(8,128)S(1)} collective-permute-done((f32[72,128]{1,0:T(8,128)S(1)}, f32[72,128]{1,0:T(8,128)S(1)}, u32[]{:S(2)}, u32[]{:S(2)}) %collective-permute-start.5) | collective-permute-done | bytes 36896 | tf_op jit(solution)/shard_map/ppermute | solution.py:214
  26.3 0.0 collective-permute-done.4.refs_1_
  26.3 0.0 copy-done
  26.3 0.4 %shard_map.59 = f32[4,256]{1,0:T(4,128)S(1)} custom-call(f32[72,128]{1,0:T(8,128)S(1)} %shard_map.58.refs_0_, f32[72,128]{1,0:T(8,128)S(1)} %collective-permute-done.4.refs_1_, f32[72,128]{1,0:T(8,128)S(1)} %collective-permute-done.5.refs_2_, f32[72,128]{1,0:T(8,128)S(1)} %collective-permute-done.6.refs_3_, bf16[2048,256]{1,0:T(8,128)(2,1)S(1)} %copy-done), custom_call_target="tpu_custom_call" | custom-call | tf_op jit(solution)/shard_map/pallas_call | solution.py:202
  26.7 3.9 %collective-permute-start.9 = (f32[4,256]{1,0:T(4,128)S(1)}, f32[4,256]{1,0:T(4,128)S(1)}, u32[]{:S(2)}, u32[]{:S(2)}) collective-permute-start(f32[4,256]{1,0:T(4,128)S(1)} %shard_map.59), channel_id=1, source_target_pairs={{0,2},{1,3},{2,0},{3,1},{4,6},{5,7},{6,4},{7,5},{8,10},{9,11},{10,... | collective-permute-start | bytes 12296 | tf_op jit(solution)/shard_map/ppermute | solution.py:214
  30.6 0.7 %collective-permute-start.8 = (f32[4,256]{1,0:T(4,128)S(1)}, f32[4,256]{1,0:T(4,128)S(1)}, u32[]{:S(2)}, u32[]{:S(2)}) collective-permute-start(f32[4,256]{1,0:T(4,128)S(1)} %shard_map.59), channel_id=1, source_target_pairs={{0,3},{1,2},{2,1},{3,0},{4,7},{5,6},{6,5},{7,4},{8,11},{9,10},{10,... | collective-permute-start | bytes 12296 | tf_op jit(solution)/shard_map/ppermute | solution.py:214
  31.3 0.3 collective-permute-start.7
  31.6 0.6 %collective-permute-done.9 = f32[4,256]{1,0:T(4,128)S(1)} collective-permute-done((f32[4,256]{1,0:T(4,128)S(1)}, f32[4,256]{1,0:T(4,128)S(1)}, u32[]{:S(2)}, u32[]{:S(2)}) %collective-permute-start.9) | collective-permute-done | bytes 4128 | tf_op jit(solution)/shard_map/ppermute | solution.py:214
  32.2 3.2 %collective-permute-done.8 = f32[4,256]{1,0:T(4,128)S(1)} collective-permute-done((f32[4,256]{1,0:T(4,128)S(1)}, f32[4,256]{1,0:T(4,128)S(1)}, u32[]{:S(2)}, u32[]{:S(2)}) %collective-permute-start.8) | collective-permute-done | bytes 4128 | tf_op jit(solution)/shard_map/ppermute | solution.py:214
  35.4 0.0 collective-permute-done.7
  35.4 0.6 %add_add_fusion = f32[4,256]{1,0:T(4,128)} fusion(f32[4,256]{1,0:T(4,128)S(1)} %collective-permute-done.9, f32[4,256]{1,0:T(4,128)S(1)} %collective-permute-done.8, f32[4,256]{1,0:T(4,128)S(1)} %shard_map.59, f32[4,256]{1,0:T(4,128)S(1)} %collective-permute-done.7), kind=kLoop, calls=%fused_computation | loop fusion | flops 3072 | bytes 20480 | tf_op jit(solution)/shard_map/add | solution.py:223
  (3 shorter events, 0.1 us)
Async XLA Ops:
  0.0 26.3 %copy-start = (bf16[2048,256]{1,0:T(8,128)(2,1)S(1)}, bf16[2048,256]{1,0:T(8,128)(2,1)}, u32[]{:S(2)}) copy-start(bf16[2048,256]{1,0:T(8,128)(2,1)} %refs_4_.1) | copy-start | bytes 3145732
  7.9 1.5 %collective-permute-start = (f32[72,128]{1,0:T(8,128)}, f32[72,128]{1,0:T(8,128)S(1)}, u32[]{:S(2)}, u32[]{:S(2)}) collective-permute-start(f32[72,128]{1,0:T(8,128)} %shard_map.55.source), channel_id=1, source_target_pairs={{0,4},{4,0},{8,12},{12,8},{16,20},{20,16},{24,28},{28,24},{32,36},... | collective-permute-start | bytes 110600 | tf_op jit(solution)/shard_map/ppermute | solution.py:214
  8.0 0.8 %copy-start.1 = (f32[72,128]{1,0:T(8,128)S(1)}, f32[72,128]{1,0:T(8,128)}, u32[]{:S(2)}) copy-start(f32[72,128]{1,0:T(8,128)} %shard_map.55.source) | copy-start | bytes 110596
  9.5 5.5 %collective-permute-start.3 = (f32[72,128]{1,0:T(8,128)S(1)}, f32[72,128]{1,0:T(8,128)S(1)}, u32[]{:S(2)}, u32[]{:S(2)}) collective-permute-start(f32[72,128]{1,0:T(8,128)S(1)} %shard_map.57.refs_0_), channel_id=1, source_target_pairs={{0,16},{4,20},{8,24},{12,28},{16,0},{20,4},{24,8},{28,12},{32,48},... | collective-permute-start | bytes 110600 | tf_op jit(solution)/shard_map/ppermute | solution.py:214
  12.8 5.2 %collective-permute-start.2 = (f32[72,128]{1,0:T(8,128)S(1)}, f32[72,128]{1,0:T(8,128)S(1)}, u32[]{:S(2)}, u32[]{:S(2)}) collective-permute-start(f32[72,128]{1,0:T(8,128)S(1)} %shard_map.57.refs_0_), channel_id=1, source_target_pairs={{0,24},{4,28},{8,16},{12,20},{16,8},{20,12},{24,0},{28,4},{32,56},... | collective-permute-start | bytes 110600 | tf_op jit(solution)/shard_map/ppermute | solution.py:214
  13.9 4.1 %collective-permute-start.1 = (f32[72,128]{1,0:T(8,128)S(1)}, f32[72,128]{1,0:T(8,128)S(1)}, u32[]{:S(2)}, u32[]{:S(2)}) collective-permute-start(f32[72,128]{1,0:T(8,128)S(1)} %shard_map.57.refs_0_), channel_id=1, source_target_pairs={{0,8},{4,12},{8,0},{12,4},{16,24},{20,28},{24,16},{28,20},{32,40},... | collective-permute-start | bytes 110600 | tf_op jit(solution)/shard_map/ppermute | solution.py:214
  18.0 5.6 %collective-permute-start.6 = (f32[72,128]{1,0:T(8,128)S(1)}, f32[72,128]{1,0:T(8,128)S(1)}, u32[]{:S(2)}, u32[]{:S(2)}) collective-permute-start(f32[72,128]{1,0:T(8,128)S(1)} %shard_map.58.refs_0_), channel_id=1, source_target_pairs={{0,64},{4,68},{8,72},{12,76},{16,80},{20,84},{24,88},{28,92},{32,9... | collective-permute-start | bytes 110600 | tf_op jit(solution)/shard_map/ppermute | solution.py:214
  21.1 5.2 %collective-permute-start.5 = (f32[72,128]{1,0:T(8,128)S(1)}, f32[72,128]{1,0:T(8,128)S(1)}, u32[]{:S(2)}, u32[]{:S(2)}) collective-permute-start(f32[72,128]{1,0:T(8,128)S(1)} %shard_map.58.refs_0_), channel_id=1, source_target_pairs={{0,96},{4,100},{8,104},{12,108},{16,112},{20,116},{24,120},{28,124... | collective-permute-start | bytes 110600 | tf_op jit(solution)/shard_map/ppermute | solution.py:214
  22.3 4.0 %collective-permute-start.4 = (f32[72,128]{1,0:T(8,128)S(1)}, f32[72,128]{1,0:T(8,128)S(1)}, u32[]{:S(2)}, u32[]{:S(2)}) collective-permute-start(f32[72,128]{1,0:T(8,128)S(1)} %shard_map.58.refs_0_), channel_id=1, source_target_pairs={{0,32},{4,36},{8,40},{12,44},{16,48},{20,52},{24,56},{28,60},{32,0... | collective-permute-start | bytes 110600 | tf_op jit(solution)/shard_map/ppermute | solution.py:214
  26.7 5.5 %collective-permute-start.9 = (f32[4,256]{1,0:T(4,128)S(1)}, f32[4,256]{1,0:T(4,128)S(1)}, u32[]{:S(2)}, u32[]{:S(2)}) collective-permute-start(f32[4,256]{1,0:T(4,128)S(1)} %shard_map.59), channel_id=1, source_target_pairs={{0,2},{1,3},{2,0},{3,1},{4,6},{5,7},{6,4},{7,5},{8,10},{9,11},{10,... | collective-permute-start | bytes 12296 | tf_op jit(solution)/shard_map/ppermute | solution.py:214
  30.6 4.8 %collective-permute-start.8 = (f32[4,256]{1,0:T(4,128)S(1)}, f32[4,256]{1,0:T(4,128)S(1)}, u32[]{:S(2)}, u32[]{:S(2)}) collective-permute-start(f32[4,256]{1,0:T(4,128)S(1)} %shard_map.59), channel_id=1, source_target_pairs={{0,3},{1,2},{2,1},{3,0},{4,7},{5,6},{6,5},{7,4},{8,11},{9,10},{10,... | collective-permute-start | bytes 12296 | tf_op jit(solution)/shard_map/ppermute | solution.py:214
  31.3 4.1 %collective-permute-start.7 = (f32[4,256]{1,0:T(4,128)S(1)}, f32[4,256]{1,0:T(4,128)S(1)}, u32[]{:S(2)}, u32[]{:S(2)}) collective-permute-start(f32[4,256]{1,0:T(4,128)S(1)} %shard_map.59), channel_id=1, source_target_pairs={{0,1},{1,0},{2,3},{3,2},{4,5},{5,4},{6,7},{7,6},{8,9},{9,8},{10,11... | collective-permute-start | bytes 12296 | tf_op jit(solution)/shard_map/ppermute | solution.py:214
